TPU v7x, 512 devices: a whole 4x4x16 slice. The times are simulated.
512 devices in a mesh: seq: 64 (over y, z), head: 8 (over x, core).
Axes of the slice: x: 4, y: 4, z: 16, core: 2. Of those that a mesh axis runs over, the one named last changes fastest.
Arguments:
- queries: bfloat16 [128, 4096], P(None, 'head'), may hold values from -400 to 400
- keys: bfloat16 [16384, 1024], P('seq', 'head'), may hold values from -6 to 6
- values: bfloat16 [16384, 1024], P('seq', 'head'), may hold values from -6 to 6
- householder: bfloat16 [16384, 1024], P('seq', 'head'), may hold values from -6 to 6
- out_proj: bfloat16 [4096, 4096], P('head', 'seq'), may hold values from -0.09375 to 0.09375
Outputs:
- mixed: bfloat16 [128, 4096], P('head', 'seq')
All inputs are finite; a program needn't handle non-finite values.
Results may differ from a plain program's by a relative error of at most 0.02.
Values may be sent and summed in bfloat16 or wider, within the bound.
A program may use at most 64 MiB of HBM per device.

v0:
```python
import jax
import jax.numpy as jnp
from jax import lax
from jax.sharding import PartitionSpec as P

BLOCK = 64


def merged(array, axis, combine):
    everything = jax.tree.map(lambda part: lax.all_gather(part, axis), array)
    initial = jax.tree.map(lambda part: part[0], everything)

    def turn(k, so_far):
        return combine(so_far, jax.tree.map(lambda part: part[k], everything))

    return lax.fori_loop(1, lax.axis_size(axis), turn, initial)


def unit_rows(raw_vecs):
    return raw_vecs * lax.rsqrt(jnp.sum(raw_vecs * raw_vecs, axis=-1, keepdims=True) + 1e-06)


def span_forms(raw_vecs, keys_float):
    precise = lax.Precision.HIGHEST
    vectors = unit_rows(raw_vecs)
    block_len = vectors.shape[1]
    head_width = vectors.shape[2]
    row_ids = lax.broadcasted_iota(jnp.int32, (block_len, block_len), 0)
    col_ids = lax.broadcasted_iota(jnp.int32, (block_len, block_len), 1)
    gram = jnp.einsum("nad,nbd->nab", vectors, vectors, precision=precise)
    lower = jnp.where(row_ids > col_ids, gram, 0.0) + jnp.where(row_ids == col_ids, 0.5, 0.0)
    identity_block = jnp.broadcast_to(jnp.eye(block_len, dtype=jnp.float32), lower.shape)
    coeff = jax.scipy.linalg.solve_triangular(lower, identity_block, lower=True)
    identity_head = jnp.eye(head_width, dtype=jnp.float32)
    transition = identity_head - jnp.einsum(
        "nad,nab,nbe->nde", vectors, coeff, vectors, precision=precise
    )
    inner = jnp.einsum("nbd,njd->nbj", vectors, keys_float, precision=precise)
    inner = jnp.where(row_ids > col_ids, inner, 0.0)
    mixing = jnp.einsum("nab,nbj->naj", coeff, inner, precision=precise)
    carried = keys_float - jnp.einsum("naj,nad->njd", mixing, vectors, precision=precise)
    return (transition, carried)


def carry_back(transition, carried, identity_head):
    precise = lax.Precision.HIGHEST

    def advance(running, span_item):
        factor, block_keys = span_item
        emitted = jnp.dot(block_keys, running.T, precision=precise)
        return (jnp.dot(running, factor, precision=precise), emitted)

    return lax.scan(advance, identity_head, (transition, carried), reverse=True)


def compose_batch(earlier, later):
    return jnp.einsum("nab,nbc->nac", earlier, later, precision=lax.Precision.HIGHEST)


def combine_parts(first, second):
    peak_one, total_one, numer_one = first
    peak_two, total_two, numer_two = second
    peak = jnp.maximum(peak_one, peak_two)
    factor_one = jnp.exp(peak_one - peak)
    factor_two = jnp.exp(peak_two - peak)
    return (
        peak,
        total_one * factor_one + total_two * factor_two,
        numer_one * factor_one[..., None] + numer_two * factor_two[..., None],
    )


def on_device(queries, keys, values, householder, out_proj):
    precise = lax.Precision.HIGHEST
    ctx_rows, head_width = keys.shape
    blocks = ctx_rows // BLOCK
    raw_vecs = householder.astype(jnp.float32).reshape(blocks, BLOCK, head_width)
    keys_float = keys.astype(jnp.float32).reshape(blocks, BLOCK, head_width)
    transition, carried = span_forms(raw_vecs, keys_float)
    identity_head = jnp.eye(head_width, dtype=jnp.float32)
    shard_mat, local_keys = carry_back(transition, carried, identity_head)
    local_keys = local_keys.reshape(ctx_rows, head_width)
    all_trans = lax.all_gather(shard_mat[None], "seq", axis=0, tiled=True)
    my_index = lax.axis_index("seq")
    inclusive = lax.associative_scan(compose_batch, all_trans, reverse=True)
    padded_stack = jnp.concatenate([inclusive, identity_head[None]], axis=0)
    suffix_mat = lax.dynamic_index_in_dim(padded_stack, my_index + 1, 0, keepdims=False)
    query_count = queries.shape[0]
    group_size = queries.shape[1] // head_width
    query_float = queries.astype(jnp.float32).reshape(query_count, group_size, head_width)
    turned = jnp.einsum("ihe,ef->hif", query_float, suffix_mat, precision=precise)
    inv_root = 1.0 / jnp.sqrt(jnp.float32(head_width))

    def attend(query_rows):
        scores = jnp.einsum("if,jf->ij", query_rows, local_keys, precision=precise) * inv_root
        peak = jnp.max(scores, axis=1)
        expo = jnp.exp(scores - peak[:, None])
        totals = jnp.sum(expo, axis=1)
        numerators = jnp.dot(expo.astype(jnp.bfloat16), values, preferred_element_type=jnp.float32)
        return (peak, totals, numerators)

    peaks, totals, numerators = lax.map(attend, turned)
    best, merged_total, merged_numer = merged((peaks, totals, numerators), "seq", combine_parts)
    attention = (merged_numer / merged_total[..., None]).astype(jnp.bfloat16)
    flat_attention = jnp.transpose(attention, (1, 0, 2)).reshape(
        query_count, group_size * head_width
    )
    return lax.psum_scatter(
        jnp.dot(flat_attention, out_proj, preferred_element_type=jnp.float32).astype(jnp.bfloat16),
        "head",
        scatter_dimension=0,
        tiled=True,
    )


def solution(mesh):
    placed = (
        P(None, "head"),
        P("seq", "head"),
        P("seq", "head"),
        P("seq", "head"),
        P("head", "seq"),
    )
    return jax.shard_map(
        on_device, mesh=mesh, in_specs=placed, out_specs=P("head", "seq"), check_vma=False
    )
```

profile of v0, /device:TPU:8, one launch (start us, length us, event | category | flops | bytes accessed | tf_op | source)
XLA Modules:
  0.0 596.8 jit_solution(18420621423005850482)
XLA Ops:
  7.8 1.3 fusion.24
  9.1 19.7 %custom-call.4 = f32[4,1,64,64]{2,3,1,0:T(8,128)S(1)} custom-call(f32[4,1,64,64]{3,2,1,0:T(8,128)S(1)} %fusion.24), custom_call_target="InvertDiagBlocksLowerTriangular" | custom-call | tf_op jit(solution)/shard_map/jit(_solve_triangular)/vmap()/triangular_solve | solution.py:33
  30.3 1.3 fusion.50
  32.0 1.2 convolution_subtract_fusion.1
  33.9 2.1 while.49
  36.9 149.7 %all-gather.9.cloned.1.call-done = f32[8192,128]{1,0:T(8,128)} async-done(((f32[128,128]{1,0:T(8,128)}), f32[8192,128]{1,0:T(8,128)}) %all-gather.9.cloned.1.call-update) | async-done | bytes 4194320 | tf_op jit(solution)/shard_map/all_gather | solution.py:83
  186.6 3.1 slice.111
  189.8 1.7 slice.112
  191.5 3.7 fusion.18
  200.7 5.8 pad.43
  206.5 1.3 add.157
  210.0 10.2 %pad.46 = f32[32,128,128]{2,1,0:T(8,128)} pad(f32[16,128,128]{2,1,0:T(8,128)} %copy-done.3, f32[]{:T(128)} %constant.115.clone.1), padding=1_0_1x0_0_0x0_0_0 | pad | bytes 3145732 | tf_op jit(solution)/shard_map/pad | solution.py:85
  220.2 6.5 %pad.45 = f32[32,128,128]{2,1,0:T(8,128)} pad(f32[16,128,128]{2,1,0:T(8,128)S(1)} %pad_maximum_fusion.1, f32[]{:T(128)} %constant.115.clone.1), padding=0_1_1x0_0_0x0_0_0 | pad | bytes 3145732 | tf_op jit(solution)/shard_map/pad | solution.py:85
  226.7 2.5 add.158
  229.2 5.0 fusion.20
  234.2 12.1 %pad.48 = f32[64,128,128]{2,1,0:T(8,128)} pad(f32[32,128,128]{2,1,0:T(8,128)S(1)} %add.158, f32[]{:T(128)} %constant.115.clone.1), padding=1_0_1x0_0_0x0_0_0 | pad | bytes 6291460 | tf_op jit(solution)/shard_map/pad | solution.py:85
  247.1 1.7 pad_maximum_fusion
  248.8 12.1 %pad.47 = f32[64,128,128]{2,1,0:T(8,128)} pad(f32[32,128,128]{2,1,0:T(8,128)S(1)} %pad_maximum_fusion, f32[]{:T(128)} %constant.115.clone.1), padding=0_1_1x0_0_0x0_0_0 | pad | bytes 6291460 | tf_op jit(solution)/shard_map/pad | solution.py:85
  260.9 6.5 %add.159 = f32[64,128,128]{2,1,0:T(8,128)} add(f32[64,128,128]{2,1,0:T(8,128)} %pad.47, f32[64,128,128]{2,1,0:T(8,128)} %pad.48) | non-fusion elementwise | flops 1048576 | bytes 12582912 | tf_op jit(solution)/shard_map/add | solution.py:85
  267.4 4.6 rev.4
  273.3 6.0 %while.50 = (s32[]{:T(128)}, f32[4,128]{1,0:T(4,128)S(1)}, f32[4,128]{1,0:T(4,128)S(1)}, f32[4,128,128]{2,1,0:T(8,128)}, f32[4,128,128]{1,2,0:T(8,128)S(1)}, /*i...) while((s32[]{:T(128)}, f32[4,128]{1,0:T(4,128)S(1)}, ...), condition=%wide.region_6.7_spmd, body=%wide.region_3.6_spmd.sunk | while | flops 58916608 | bytes 725109 | solution.py:102
  279.3 97.9 %all-gather.4 = f32[64,4,128]{2,1,0:T(4,128)S(1)} all-gather(f32[1,4,128]{2,1,0:T(4,128)S(1)} %bitcast.152), channel_id=3, replica_groups=mesh['seq'=64,'head'=8] {'seq'}, dimensions={0}, use_global_device_ids=true | all-gather | bytes 133120 | tf_op jit(solution)/shard_map/all_gather | solution.py:10
  377.2 98.0 %all-gather.5 = f32[64,4,128]{2,1,0:T(4,128)S(1)} all-gather(f32[1,4,128]{2,1,0:T(4,128)S(1)} %bitcast.151), channel_id=4, replica_groups=mesh['seq'=64,'head'=8] {'seq'}, dimensions={0}, use_global_device_ids=true | all-gather | bytes 133120 | tf_op jit(solution)/shard_map/all_gather | solution.py:10
  476.2 79.3 %while.51 = (s32[]{:T(128)}, f32[4,128]{1,0:T(4,128)S(1)}, f32[4,128]{1,0:T(4,128)S(1)}, f32[4,128,128]{2,1,0:T(8,128)S(1)}, f32[64,4,128]{2,1,0:T(4,128)S(1)}, ...) while((s32[]{:T(128)}, f32[4,128]{1,0:T(4,128)S(1)}, ...), condition=%wide.region_8.9_spmd, body=%wide.region_7.8_spmd.sunk | while | flops 199685 | bytes 807055 | solution.py:16
  476.3 1.2 fusion.125
  477.5 1.2 fusion.125
  478.8 1.2 fusion.125
  480.0 1.2 fusion.125
  481.3 1.2 fusion.125
  482.6 1.2 fusion.125
  483.8 1.2 fusion.125
  485.1 1.2 fusion.125
  486.3 1.2 fusion.125
  492.6 1.2 fusion.125
  493.9 1.2 fusion.125
  495.1 1.2 fusion.125
  496.4 1.2 fusion.125
  497.7 1.2 fusion.125
  498.9 1.2 fusion.125
  500.2 1.2 fusion.125
  501.4 1.2 fusion.125
  502.7 1.2 fusion.125
  503.9 1.2 fusion.125
  505.2 1.2 fusion.125
  506.5 1.2 fusion.125
  507.7 1.2 fusion.125
  509.0 1.2 fusion.125
  510.2 1.2 fusion.125
  516.5 1.2 fusion.125
  517.8 1.2 fusion.125
  519.0 1.2 fusion.125
  520.3 1.2 fusion.125
  521.6 1.2 fusion.125
  522.8 1.2 fusion.125
  524.1 1.2 fusion.125
  525.3 1.2 fusion.125
  526.6 1.2 fusion.125
  527.9 1.2 fusion.125
  529.1 1.2 fusion.125
  530.4 1.2 fusion.125
  531.6 1.2 fusion.125
  532.9 1.2 fusion.125
  534.1 1.2 fusion.125
  556.6 33.7 %reduce-scatter.2.cloned.1.call-done = bf16[16,64]{1,0:T(8,128)(2,1)} async-done(((bf16[128,64]{1,0:T(8,128)(2,1)}), bf16[16,64]{1,0:T(8,128)(2,1)}) %reduce-scatter.2.cloned.1.call-update) | async-done | bytes 2064 | tf_op jit(solution)/shard_map/reduce_scatter | solution.py:108
  (193 shorter events, 54.9 us)
Async XLA Ops:
  6.5 265.5 %copy-start = (bf16[128,512]{1,0:T(8,128)(2,1)S(1)}, bf16[128,512]{1,0:T(8,128)(2,1)}, u32[]{:S(2)}) copy-start(bf16[128,512]{1,0:T(8,128)(2,1)} %param.11) | copy-start | bytes 393220
  6.5 26.7 %copy-start.4 = (bf16[256,128]{1,0:T(8,128)(2,1)S(1)}, bf16[256,128]{1,0:T(8,128)(2,1)}, u32[]{:S(2)}) copy-start(bf16[256,128]{1,0:T(8,128)(2,1)} %param.14) | copy-start | bytes 196612
  6.5 180.1 %all-gather.9.cloned.1.call-start = ((), (), s32[]{:S(2)}) async-start(), calls=%async_computation.2 | async-start | bytes 4259840 | tf_op jit(solution)/shard_map/all_gather | solution.py:83
  36.8 438.4 %all-gather.11.cloned.1.call-start = ((), (), s32[]{:S(2)}) async-start(), calls=%async_computation.3 | async-start | bytes 17039360 | tf_op jit(solution)/shard_map/all_gather | solution.py:10
  195.2 1.9 copy-start.1
  200.7 8.2 %copy-start.2 = (f32[32,128,128]{2,1,0:T(8,128)S(1)}, f32[32,128,128]{2,1,0:T(8,128)}, u32[]{:S(2)}) copy-start(f32[32,128,128]{2,1,0:T(8,128)} %copy-done.1) | copy-start | bytes 6291460
  207.8 1.1 copy-start.3
  210.0 10.2 %slice-start = ((f32[32,128,128]{2,1,0:T(8,128)}), f32[1,128,128]{2,1,0:T(8,128)S(1)}, s32[]{:S(2)}) async-start(f32[32,128,128]{2,1,0:T(8,128)} %copy-done.1), calls=%async_computation.4 | async-start | bytes 131072 | tf_op jit(solution)/shard_map/slice | solution.py:85
  272.1 1.2 copy-start.5
  279.3 310.9 %reduce-scatter.2.cloned.1.call-start = ((), (), s32[]{:S(2)}) async-start(), calls=%async_computation.1 | async-start | bytes 36864 | tf_op jit(solution)/shard_map/reduce_scatter | solution.py:108
  476.2 79.5 %copy-start.6 = (bf16[512,64]{0,1:T(8,128)(2,1)S(1)}, bf16[512,64]{0,1:T(8,128)(2,1)}, u32[]{:S(2)}) copy-start(bf16[512,64]{0,1:T(8,128)(2,1)} %param.15) | copy-start | bytes 196612
Sparse Core Ops, SparseCore 0:
  36.9 149.6 all-gather.8
  279.4 188.8 all-gather.10
  556.7 33.5 reduce-scatter.1
where the time goes:
time: 600 us; the launch traced here: 597 us
  blocking collectives  196 us (33%)
  waiting for transfers between devices  183 us (30%)
  other arithmetic  112 us (19%)
  local copies, waits for them, and re-layouts  60.8 us (10%)
  matrix products  28.9 us (5%)
  between operations  13.6 us (2%)
    all_gather x2, blocking collectives, merged(): everything = jax.tree.map(lambda part: lax.all_gather(part, axis), array)  196 us
    all_gather x1, waiting for transfers between devices, on_device(): all_trans = lax.all_gather(shard_mat[None], 'seq', axis=0, tiled=True)  150 us
    add x63, other arithmetic, combine_parts(): numer_one * factor_one[..., None] + numer_two * factor_two[..., None]  76 us
    pad x10, local copies, waits for them, and re-layouts, on_device(): inclusive = lax.associative_scan(compose_batch, all_trans, reverse=True)  47.1 us
    reduce_scatter x1, waiting for transfers between devices, on_device(): lax.psum_scatter(jnp.dot(flat_attention, out_proj, preferred_element_type...  33.7 us
    another operation x1, other arithmetic, span_forms(): coeff = jax.scipy.linalg.solve_triangular(lower, identity_block, lower=True)  19.7 us
    dot_general x11, matrix products, compose_batch(): jnp.einsum('nab,nbc->nac', earlier, later, precision=lax.Precision.HIGHEST)  13.6 us
  transfers between devices with their start and end apart: 3, of which 2 were waited for; matrix products, arithmetic and copies ran while one was open for 0% of the time, Pallas kernels for 0%

commit v1 on v0

--- a/solution.py
+++ b/solution.py
@@ -80,7 +80,9 @@
     identity_head = jnp.eye(head_width, dtype=jnp.float32)
     shard_mat, local_keys = carry_back(transition, carried, identity_head)
     local_keys = local_keys.reshape(ctx_rows, head_width)
-    all_trans = lax.all_gather(shard_mat[None], "seq", axis=0, tiled=True)
+    all_trans = jnp.concatenate(
+        lax.all_to_all(jnp.stack([shard_mat[None]] * lax.axis_size("seq")), "seq", 0, 0), axis=0
+    )
     my_index = lax.axis_index("seq")
     inclusive = lax.associative_scan(compose_batch, all_trans, reverse=True)
     padded_stack = jnp.concatenate([inclusive, identity_head[None]], axis=0)

time: 600 us -> 657 us (1.095)
  waiting for transfers between devices: 183 us -> 218 us
  starting transfers between devices: 0.09 us -> 19 us
    all_to_all x0 -> x1, waiting for transfers between devices: none -> 185 us  [on_device(): lax.all_to_all(jnp.stack([shard_mat[None]] * lax.axis_size('seq')), 'seq'...]
    all_gather x1 -> x0, waiting for transfers between devices: 150 us -> none  [on_device(): all_trans = lax.all_gather(shard_mat[None], 'seq', axis=0, tiled=True)]
    all_to_all x0 -> x1, starting transfers between devices: none -> 18.9 us  [on_device(): lax.all_to_all(jnp.stack([shard_mat[None]] * lax.axis_size('seq')), 'seq'...]
where the time goes in v1:
time: 657 us; the launch traced here: 653 us
  waiting for transfers between devices  218 us (33%)
  blocking collectives  197 us (30%)
  other arithmetic  112 us (17%)
  local copies, waits for them, and re-layouts  62.2 us (9%)
  matrix products  28.9 us (4%)
  starting transfers between devices  19 us (3%)
  between operations  13.9 us (2%)
    all_gather x2, blocking collectives, merged(): everything = jax.tree.map(lambda part: lax.all_gather(part, axis), array)  197 us
    all_to_all x1, waiting for transfers between devices, on_device(): lax.all_to_all(jnp.stack([shard_mat[None]] * lax.axis_size('seq')), 'seq'...  185 us
    add x63, other arithmetic, combine_parts(): numer_one * factor_one[..., None] + numer_two * factor_two[..., None]  76 us
    pad x10, local copies, waits for them, and re-layouts, on_device(): inclusive = lax.associative_scan(compose_batch, all_trans, reverse=True)  46.6 us
    reduce_scatter x1, waiting for transfers between devices, on_device(): lax.psum_scatter(jnp.dot(flat_attention, out_proj, preferred_element_type...  32.9 us
    another operation x1, other arithmetic, span_forms(): coeff = jax.scipy.linalg.solve_triangular(lower, identity_block, lower=True)  19.7 us
    all_to_all x1, starting transfers between devices, on_device(): lax.all_to_all(jnp.stack([shard_mat[None]] * lax.axis_size('seq')), 'seq'...  18.9 us
    dot_general x11, matrix products, compose_batch(): jnp.einsum('nab,nbc->nac', earlier, later, precision=lax.Precision.HIGHEST)  13.6 us
  transfers between devices with their start and end apart: 3, of which 2 were waited for; matrix products, arithmetic and copies ran while one was open for 0% of the time, Pallas kernels for 0%

profile of v1, /device:TPU:8, one launch (start us, length us, event | category | flops | bytes accessed | tf_op | source)
XLA Modules:
  0.0 653.1 jit_solution(17366369527711899491)
XLA Ops:
  7.8 1.3 fusion.24
  9.1 19.7 %custom-call.4 = f32[4,1,64,64]{2,3,1,0:T(8,128)S(1)} custom-call(f32[4,1,64,64]{3,2,1,0:T(8,128)S(1)} %fusion.24), custom_call_target="InvertDiagBlocksLowerTriangular" | custom-call | tf_op jit(solution)/shard_map/jit(_solve_triangular)/vmap()/triangular_solve | solution.py:33
  30.3 1.3 fusion.50
  32.0 1.2 convolution_subtract_fusion.1
  33.9 2.1 while.49
  36.1 2.5 stack.3
  38.6 18.9 %all-to-all-start = ((f32[64,1,128,128]{3,2,1,0:T(8,128)}), f32[64,1,128,128]{3,2,1,0:T(8,128)}, u32[]{:S(2)}, u32[]{:S(2)}) async-start(f32[64,1,128,128]{3,2,1,0:T(8,128)} %stack.3), calls=%async_computation | async-start | bytes 8388608 | tf_op jit(solution)/shard_map/all_to_all | solution.py:84
  57.7 185.3 %all-to-all-done = f32[64,1,128,128]{3,2,1,0:T(8,128)} async-done(((f32[64,1,128,128]{3,2,1,0:T(8,128)}), f32[64,1,128,128]{3,2,1,0:T(8,128)}, u32[]{:S(2)}, u32[]{:S(2)}) %all-to-all-start) | async-done | bytes 4194336 | tf_op jit(solution)/shard_map/all_to_all | solution.py:84
  243.0 3.1 slice.115
  246.1 1.7 slice.116
  247.9 3.7 fusion.18
  257.1 5.7 pad.43
  262.8 1.3 add.157
  266.3 10.1 %pad.46 = f32[32,128,128]{2,1,0:T(8,128)} pad(f32[16,128,128]{2,1,0:T(8,128)} %copy-done.3, f32[]{:T(128)} %constant.115.clone.1), padding=1_0_1x0_0_0x0_0_0 | pad | bytes 3145732 | tf_op jit(solution)/shard_map/pad | solution.py:87
  276.6 6.3 pad.45
  282.9 2.5 add.158
  285.4 5.0 fusion.20
  290.3 12.0 %pad.48 = f32[64,128,128]{2,1,0:T(8,128)} pad(f32[32,128,128]{2,1,0:T(8,128)S(1)} %add.158, f32[]{:T(128)} %constant.115.clone.1), padding=1_0_1x0_0_0x0_0_0 | pad | bytes 6291460 | tf_op jit(solution)/shard_map/pad | solution.py:87
  303.1 1.7 pad_maximum_fusion
  304.8 11.9 %pad.47 = f32[64,128,128]{2,1,0:T(8,128)} pad(f32[32,128,128]{2,1,0:T(8,128)S(1)} %pad_maximum_fusion, f32[]{:T(128)} %constant.115.clone.1), padding=0_1_1x0_0_0x0_0_0 | pad | bytes 6291460 | tf_op jit(solution)/shard_map/pad | solution.py:87
  316.8 6.5 add.159
  323.3 4.6 rev.4
  329.1 6.0 while.50
  335.2 99.5 %all-gather.3 = f32[64,4,128]{2,1,0:T(4,128)S(1)} all-gather(f32[1,4,128]{2,1,0:T(4,128)S(1)} %bitcast.149), channel_id=2, replica_groups=mesh['seq'=64,'head'=8] {'seq'}, dimensions={0}, use_global_device_ids=true | all-gather | bytes 133120 | tf_op jit(solution)/shard_map/all_gather | solution.py:10
  434.8 97.4 %all-gather.4 = f32[64,4,128]{2,1,0:T(4,128)S(1)} all-gather(f32[1,4,128]{2,1,0:T(4,128)S(1)} %bitcast.148), channel_id=3, replica_groups=mesh['seq'=64,'head'=8] {'seq'}, dimensions={0}, use_global_device_ids=true | all-gather | bytes 133120 | tf_op jit(solution)/shard_map/all_gather | solution.py:10
  533.2 79.1 %while.51 = (s32[]{:T(128)}, f32[4,128]{1,0:T(4,128)S(1)}, f32[4,128]{1,0:T(4,128)S(1)}, f32[4,128,128]{2,1,0:T(8,128)S(1)}, f32[64,4,128]{2,1,0:T(4,128)S(1)}, ...) while((s32[]{:T(128)}, f32[4,128]{1,0:T(4,128)S(1)}, ...), condition=%wide.region_8.9_spmd, body=%wide.region_7.8_spmd.sunk | while | flops 199685 | bytes 807055 | solution.py:16
  533.3 1.2 fusion.125
  534.5 1.2 fusion.125
  535.8 1.2 fusion.125
  538.3 1.2 fusion.125
  539.5 1.2 fusion.125
  540.8 1.2 fusion.125
  542.1 1.2 fusion.125
  544.6 1.2 fusion.125
  545.8 1.2 fusion.125
  547.1 1.2 fusion.125
  549.6 1.2 fusion.125
  550.9 1.2 fusion.125
  552.1 1.2 fusion.125
  553.4 1.2 fusion.125
  555.9 1.2 fusion.125
  557.1 1.2 fusion.125
  558.4 1.2 fusion.125
  559.7 1.2 fusion.125
  562.2 1.2 fusion.125
  563.4 1.2 fusion.125
  564.7 1.2 fusion.125
  565.9 1.2 fusion.125
  568.4 1.2 fusion.125
  569.7 1.2 fusion.125
  571.0 1.2 fusion.125
  573.5 1.2 fusion.125
  574.7 1.2 fusion.125
  576.0 1.2 fusion.125
  577.2 1.2 fusion.125
  579.8 1.2 fusion.125
  581.0 1.2 fusion.125
  582.3 1.2 fusion.125
  583.5 1.2 fusion.125
  586.0 1.2 fusion.125
  587.3 1.2 fusion.125
  588.5 1.2 fusion.125
  589.8 1.2 fusion.125
  613.4 32.9 %reduce-scatter.2.cloned.1.call-done = bf16[16,64]{1,0:T(8,128)(2,1)} async-done(((bf16[128,64]{1,0:T(8,128)(2,1)}), bf16[16,64]{1,0:T(8,128)(2,1)}) %reduce-scatter.2.cloned.1.call-update) | async-done | bytes 2064 | tf_op jit(solution)/shard_map/reduce_scatter | solution.py:110
  (193 shorter events, 56.5 us)
Async XLA Ops:
  6.5 321.4 %copy-start = (bf16[128,512]{1,0:T(8,128)(2,1)S(1)}, bf16[128,512]{1,0:T(8,128)(2,1)}, u32[]{:S(2)}) copy-start(bf16[128,512]{1,0:T(8,128)(2,1)} %param.11) | copy-start | bytes 393220
  6.5 26.7 %copy-start.4 = (bf16[256,128]{1,0:T(8,128)(2,1)S(1)}, bf16[256,128]{1,0:T(8,128)(2,1)}, u32[]{:S(2)}) copy-start(bf16[256,128]{1,0:T(8,128)(2,1)} %param.14) | copy-start | bytes 196612
  38.6 204.4 %all-to-all-start = ((f32[64,1,128,128]{3,2,1,0:T(8,128)}), f32[64,1,128,128]{3,2,1,0:T(8,128)}, u32[]{:S(2)}, u32[]{:S(2)}) async-start(f32[64,1,128,128]{3,2,1,0:T(8,128)} %stack.3), calls=%async_computation | async-start | bytes 8388608 | tf_op jit(solution)/shard_map/all_to_all | solution.py:84
  57.5 474.7 %all-gather.7.cloned.1.call-start = ((), (), s32[]{:S(2)}) async-start(), calls=%async_computation.3 | async-start | bytes 17039360 | tf_op jit(solution)/shard_map/all_gather | solution.py:10
  251.6 1.9 copy-start.1
  257.1 8.1 %copy-start.2 = (f32[32,128,128]{2,1,0:T(8,128)S(1)}, f32[32,128,128]{2,1,0:T(8,128)}, u32[]{:S(2)}) copy-start(f32[32,128,128]{2,1,0:T(8,128)} %copy-done.1) | copy-start | bytes 6291460
  264.1 1.1 copy-start.3
  266.3 10.2 %slice-start = ((f32[32,128,128]{2,1,0:T(8,128)}), f32[1,128,128]{2,1,0:T(8,128)S(1)}, s32[]{:S(2)}) async-start(f32[32,128,128]{2,1,0:T(8,128)} %copy-done.1), calls=%async_computation.4 | async-start | bytes 131072 | tf_op jit(solution)/shard_map/slice | solution.py:87
  327.9 1.2 copy-start.5
  335.2 311.1 %reduce-scatter.2.cloned.1.call-start = ((), (), s32[]{:S(2)}) async-start(), calls=%async_computation.2 | async-start | bytes 36864 | tf_op jit(solution)/shard_map/reduce_scatter | solution.py:110
  533.2 79.3 %copy-start.6 = (bf16[512,64]{0,1:T(8,128)(2,1)S(1)}, bf16[512,64]{0,1:T(8,128)(2,1)}, u32[]{:S(2)}) copy-start(bf16[512,64]{0,1:T(8,128)(2,1)} %param.15) | copy-start | bytes 196612
Sparse Core Ops, SparseCore 0:
  335.3 188.9 all-gather.6
  613.5 32.6 reduce-scatter.1
